TPU v7x, 32 devices: a whole 2x2x4 slice. The times are simulated.
32 devices in a mesh: grp: 2 (over y), seq: 8 (over z, x), outer: 2 (over core).
Axes of the slice: x: 2, y: 2, z: 4, core: 2. Of those that a mesh axis runs over, the one named last changes fastest.
Arguments:
- keys: bfloat16 [4096, 512], P(('grp', 'seq', 'outer')), parts along dimension 0, may hold values from -6 to 6
- values: bfloat16 [4096, 512], P(('grp', 'seq', 'outer')), parts along dimension 0, may hold values from -6 to 6
- queries: bfloat16 [4096, 512], P(('grp', 'seq', 'outer')), parts along dimension 0, may hold values from -6 to 6
- learn_rate: float32 [4096], P(('grp', 'seq', 'outer')), parts along dimension 0, may hold values from 0.0006629126 to 0.006629126
- w_gate: bfloat16 [1024, 512], P('grp'), parts along dimension 0, may hold values from -0.25 to 0.25
- w_up: bfloat16 [1024, 512], P('grp'), parts along dimension 0, may hold values from -0.25 to 0.25
- w_out: bfloat16 [1024, 512], P('grp'), parts along dimension 0, may hold values from -0.25 to 0.25
Outputs:
- output: bfloat16 [4096, 512], P(('grp', 'seq', 'outer')), parts along dimension 0
There are 2 independent parts, one for each index of `grp`. A program takes and returns all parts, laid end to end along the dimension named above; each array names one. Nothing has to cross between parts.
All inputs are finite; a program needn't handle non-finite values.
Results may differ from a plain program's by a relative error of at most 0.0098.
Values may be sent and summed in bfloat16 or wider, within the bound.
A program may use at most 64 MiB of HBM per device.

v0:
```python
import jax
import jax.numpy as jnp
from jax import lax
from jax.sharding import PartitionSpec as P

epsilon = 1e-06


def silu_grad(inputs):
    sigma = jax.nn.sigmoid(inputs)
    return sigma * (1.0 + inputs * (1.0 - sigma))


def renorm(weight, grads):
    old = weight.astype(jnp.float32)
    update = old + grads
    factor = jnp.sqrt(jnp.mean(old * old, axis=1, keepdims=True) + epsilon) / jnp.sqrt(
        jnp.mean(update * update, axis=1, keepdims=True) + epsilon
    )
    return (update * factor).astype(jnp.bfloat16)


def local(keys, values, queries, learn_rate, w_gate, w_up, w_out):
    hidden = w_gate.shape[1]
    shards = lax.axis_size(("seq", "outer"))
    rows_gate = w_gate.shape[0] // shards
    rows_out = w_out.shape[0] // shards
    position = lax.axis_index(("seq", "outer"))
    contract_last = (((1,), (1,)), ((), ()))
    contract_first = (((0,), (0,)), ((), ()))
    scaled = (learn_rate[:, None] * values.astype(jnp.float32)).astype(jnp.bfloat16)
    gate_pre = jnp.dot(keys, w_gate, preferred_element_type=jnp.float32)
    up_pre = jnp.dot(keys, w_up, preferred_element_type=jnp.float32)
    back_grad = lax.dot_general(scaled, w_out, contract_last, preferred_element_type=jnp.float32)
    activation = (jax.nn.silu(gate_pre) * up_pre).astype(jnp.bfloat16)
    d_gate = (back_grad * up_pre * silu_grad(gate_pre)).astype(jnp.bfloat16)
    d_up = (back_grad * jax.nn.silu(gate_pre)).astype(jnp.bfloat16)
    both_grads = jnp.concatenate([d_gate, d_up], axis=1)
    full_in = lax.dot_general(keys, both_grads, contract_first, preferred_element_type=jnp.float32)
    full_out = lax.dot_general(
        activation, scaled, contract_first, preferred_element_type=jnp.float32
    )
    grad_in = lax.psum_scatter(full_in, ("seq", "outer"), scatter_dimension=0, tiled=True)
    grad_out = lax.psum_scatter(full_out, ("seq", "outer"), scatter_dimension=0, tiled=True)
    own_gate = lax.dynamic_slice_in_dim(w_gate, position * rows_gate, rows_gate, 0)
    own_up = lax.dynamic_slice_in_dim(w_up, position * rows_gate, rows_gate, 0)
    own_out = lax.dynamic_slice_in_dim(w_out, position * rows_out, rows_out, 0)
    new_gate = renorm(own_gate, grad_in[:, :hidden])
    new_up = renorm(own_up, grad_in[:, hidden:])
    new_out = renorm(own_out, grad_out)
    full_gate, full_up, full_out_w = (
        lax.all_gather(new_gate, ("seq", "outer"), axis=0, tiled=True),
        lax.all_gather(new_up, ("seq", "outer"), axis=0, tiled=True),
        lax.all_gather(new_out, ("seq", "outer"), axis=0, tiled=True),
    )
    q_gate = jnp.dot(queries, full_gate, preferred_element_type=jnp.float32)
    q_up = jnp.dot(queries, full_up, preferred_element_type=jnp.float32)
    q_act = (jax.nn.silu(q_gate) * q_up).astype(jnp.bfloat16)
    return jnp.dot(q_act, full_out_w, preferred_element_type=jnp.float32).astype(jnp.bfloat16)


def solution(mesh):
    placed = (
        P(("grp", "seq", "outer"), None),
        P(("grp", "seq", "outer"), None),
        P(("grp", "seq", "outer"), None),
        P(("grp", "seq", "outer")),
        P("grp", None),
        P("grp", None),
        P("grp", None),
    )
    return jax.shard_map(
        local,
        mesh=mesh,
        in_specs=placed,
        out_specs=P(("grp", "seq", "outer"), None),
        check_vma=False,
    )
```

profile of v0, /device:TPU:0, one launch (start us, length us, event | category | flops | bytes accessed | tf_op | source)
XLA Modules:
  0.0 187.8 jit_solution(12545988453108368266)
XLA Ops:
  6.5 0.0 copy-start
  6.5 0.0 copy-start.3
  6.5 0.0 copy-start.1
  6.5 0.0 reduce-scatter.5.cloned.1.call-start
  6.5 0.9 copy-done
  7.4 1.3 fusion.21
  8.7 1.4 fusion.16
  10.2 1.4 multiply_convert_fusion.2
  11.5 0.0 copy-done.3
  11.5 0.0 copy-done.1
  11.6 1.3 fusion.11
  12.9 0.0 reduce-scatter.5.cloned.1.call-update
  12.9 0.0 reduce-scatter.7.cloned.1.call-start
  13.0 0.5 convolution_bitcast_fusion
  13.4 1.9 %copy.22 = f32[512,1024]{1,0:T(8,128)} copy(f32[512,1024]{0,1:T(8,128)S(1)} %convolution_bitcast_fusion) | data formatting | bytes 4194304
  15.3 0.0 copy-start.2
  15.3 0.0 reduce-scatter.7.cloned.1.call-update
  15.3 57.8 %reduce-scatter.5.cloned.1.call-done = f32[32,512]{1,0:T(8,128)} async-done(((f32[512,512]{1,0:T(8,128)}), f32[32,512]{1,0:T(8,128)}) %reduce-scatter.5.cloned.1.call-update) | async-done | bytes 65552 | tf_op jit(solution)/shard_map/reduce_scatter | solution.py:44
  73.1 1.0 fusion.15
  74.1 0.9 multiply_convert_fusion.5
  75.0 20.9 %all_gather.11 = bf16[512,512]{1,0:T(8,128)(2,1)S(1)} all-gather(bf16[32,512]{1,0:T(8,128)(2,1)S(1)} %multiply_convert_fusion.5), channel_id=1, replica_groups=mesh['grp'=2,'seq'=8,'outer'=2] {'seq','outer'}, dimensions={0}, use_global_device_ids=true | all-gather | bytes 557056 | tf_op jit(solution)/shard_map/all_gather | solution.py:54
  95.9 42.1 %reduce-scatter.7.cloned.1.call-done = f32[32,1024]{1,0:T(8,128)} async-done(((f32[512,1024]{1,0:T(8,128)}), f32[32,1024]{1,0:T(8,128)}) %reduce-scatter.7.cloned.1.call-update) | async-done | bytes 131088 | tf_op jit(solution)/shard_map/reduce_scatter | solution.py:43
  138.0 1.1 fusion.13
  139.1 1.0 multiply_convert_fusion.7
  140.0 20.8 %all_gather.9 = bf16[512,512]{1,0:T(8,128)(2,1)S(1)} all-gather(bf16[32,512]{1,0:T(8,128)(2,1)S(1)} %get-tuple-element.13), channel_id=1, replica_groups=mesh['grp'=2,'seq'=8,'outer'=2] {'seq','outer'}, dimensions={0}, use_global_device_ids=true | all-gather | bytes 557056 | tf_op jit(solution)/shard_map/all_gather | solution.py:52
  160.8 18.9 %all_gather.10 = bf16[512,512]{1,0:T(8,128)(2,1)S(1)} all-gather(bf16[32,512]{1,0:T(8,128)(2,1)S(1)} %get-tuple-element.14), channel_id=1, replica_groups=mesh['grp'=2,'seq'=8,'outer'=2] {'seq','outer'}, dimensions={0}, use_global_device_ids=true | all-gather | bytes 557056 | tf_op jit(solution)/shard_map/all_gather | solution.py:53
  179.7 0.0 copy-done.2
  179.7 0.2 convolution_bitcast_fusion.2
  179.9 1.1 convolution_convert_fusion
  (2 shorter events, 0.0 us)
Async XLA Ops:
  6.5 0.9 copy-start
  6.5 5.0 %copy-start.3 = (f32[128]{0:T(128)S(1)}, f32[128]{0:T(128)}, u32[]{:S(2)}) copy-start(f32[128]{0:T(128)} %param.10) | copy-start | bytes 1540
  6.5 5.0 %copy-start.1 = (bf16[128,512]{1,0:T(8,128)(2,1)S(1)}, bf16[128,512]{1,0:T(8,128)(2,1)}, u32[]{:S(2)}) copy-start(bf16[128,512]{1,0:T(8,128)(2,1)} %param.8) | copy-start | bytes 393220
  6.5 66.6 %reduce-scatter.5.cloned.1.call-start = ((), (), s32[]{:S(2)}) async-start(), calls=%async_computation.2 | async-start | bytes 1114112 | tf_op jit(solution)/shard_map/reduce_scatter | solution.py:44
  12.9 125.0 %reduce-scatter.7.cloned.1.call-start = ((), (), s32[]{:S(2)}) async-start(), calls=%async_computation.3 | async-start | bytes 2228224 | tf_op jit(solution)/shard_map/reduce_scatter | solution.py:43
  15.3 164.4 %copy-start.2 = (bf16[128,512]{1,0:T(8,128)(2,1)S(1)}, bf16[128,512]{1,0:T(8,128)(2,1)}, u32[]{:S(2)}) copy-start(bf16[128,512]{1,0:T(8,128)(2,1)} %param.9) | copy-start | bytes 393220
Sparse Core Ops, SparseCore 0:
  13.1 60.0 reduce-scatter.4
  77.3 60.6 reduce-scatter.6
where the time goes:
time: 188 us
  waiting for transfers between devices  99.9 us (53%)
  blocking collectives  60.6 us (32%)
  between operations  13.5 us (7%)
  matrix products  7.17 us (4%)
  other arithmetic  3.95 us (2%)
  local copies, waits for them, and re-layouts  2.78 us (1%)
    reduce_scatter x1, waiting for transfers between devices, local(): lax.psum_scatter(full_out, ('seq', 'outer'), scatter_dimension=0, tiled=T...  57.8 us
    reduce_scatter x1, waiting for transfers between devices, local(): lax.psum_scatter(full_in, ('seq', 'outer'), scatter_dimension=0, tiled=True)  42.1 us
    all_gather x1, blocking collectives, local(): lax.all_gather(new_out, ('seq', 'outer'), axis=0, tiled=True)  20.9 us
    all_gather x1, blocking collectives, local(): lax.all_gather(new_gate, ('seq', 'outer'), axis=0, tiled=True)  20.8 us
    all_gather x1, blocking collectives, local(): lax.all_gather(new_up, ('seq', 'outer'), axis=0, tiled=True)  18.9 us
  transfers between devices with their start and end apart: 2, of which 2 were waited for; matrix products, arithmetic and copies ran while one was open for 2% of the time, Pallas kernels for 0%

commit v1 on v0

v1 whole, which is shorter than its diff:
```python
import functools

import jax
import jax.numpy as jnp
from jax import lax
from jax.experimental import pallas as pl
from jax.experimental.pallas import tpu as pltpu
from jax.sharding import PartitionSpec as P

epsilon = 1e-06
MESH = pl.DeviceIdType.MESH
F32 = jnp.float32
BF16 = jnp.bfloat16
NT = (((1,), (1,)), ((), ()))
TN = (((0,), (0,)), ((), ()))


def silu_grad(inputs):
    sigma = jax.nn.sigmoid(inputs)
    return sigma * (1.0 + inputs * (1.0 - sigma))


def kernel(
    planes,
    lr_ref,
    k_ref,
    v_ref,
    q_ref,
    wg_ref,
    wu_ref,
    wo_ref,
    o_ref,
    kbuf,
    sbuf,
    qbuf,
    wcat,
    wback,
    old,
    acc_in,
    acc_out,
    gsend,
    grecv,
    stat,
    fact,
    wbuf,
    wq,
    wo,
    psend,
    precv,
    tok_send,
    tok_recv,
    q_send,
    q_recv,
    g_send,
    g_recv,
    st_send,
    st_recv,
    f_send,
    f_recv,
    w_send,
    w_recv,
    c_send,
    c_recv,
    p_send,
    p_recv,
):
    tokens, width = k_ref.shape
    hidden = wg_ref.shape[1]
    hb = hidden // 4
    db = width // planes
    rb = hb // planes
    spread = width // db
    seq = lax.axis_index("seq")
    core = lax.axis_index("outer")
    plane, side = seq // 2, seq % 2
    quarter = side * 2 + core
    cols = pl.ds(pl.multiple_of(quarter * hb, hb), hb)

    mate = {"outer": 1 - core}
    across = {"seq": plane * 2 + 1 - side}
    diagonal = {"seq": plane * 2 + 1 - side, "outer": 1 - core}

    def plane_at(distance):
        return (plane + distance) % planes

    def same_spot(distance):
        return {"seq": plane_at(distance) * 2 + side}

    barrier = pltpu.get_barrier_semaphore()
    peers = [mate, across, diagonal] + [same_spot(d) for d in range(1, planes)]
    for peer in peers:
        pl.semaphore_signal(barrier, inc=1, device_id=peer, device_id_type=MESH)

    def rows(slot):
        return pl.ds(slot * tokens, tokens)

    lr_cols = jnp.transpose(jnp.broadcast_to(lr_ref[...], (tokens, tokens)))
    rate = lr_cols[:, 0:1]
    sbuf[rows(0), :] = (rate * v_ref[...].astype(F32)).astype(BF16)
    kbuf[rows(0), :] = k_ref[...]
    pl.semaphore_wait(barrier, len(peers))

    def send(src, dst, send_sem, recv_sem, peer):
        copy = pltpu.make_async_remote_copy(
            src_ref=src,
            dst_ref=dst,
            send_sem=send_sem,
            recv_sem=recv_sem,
            device_id=peer,
            device_id_type=MESH,
        )
        copy.start()
        return copy

    def token_copy(buf, kind, src_slot, dst_slot, peer):
        return send(
            buf.at[rows(src_slot)],
            buf.at[rows(dst_slot)],
            tok_send.at[kind, dst_slot - 1],
            tok_recv.at[kind, dst_slot - 1],
            peer,
        )

    k_across = token_copy(kbuf, 0, 0, 2, across)
    s_across = token_copy(sbuf, 1, 0, 2, across)
    k_mate = token_copy(kbuf, 0, 0, 1, mate)
    s_mate = token_copy(sbuf, 1, 0, 1, mate)

    wcat[:, 0:hb] = wg_ref[:, cols]
    wcat[:, hb : 2 * hb] = wu_ref[:, cols]
    wback[...] = wo_ref[cols, :]

    my_cols = pl.ds(pl.multiple_of(plane * db, db), db)
    old_sums = []
    for i, ref in enumerate((wg_ref, wu_ref)):
        old[i * hb : (i + 1) * hb, :] = jnp.transpose(ref[my_cols, cols].astype(F32))
        whole = ref[my_cols, :].astype(F32)
        squares = whole * whole
        folded = squares[:, 0:hb]
        for j in range(1, 4):
            folded = folded + squares[:, j * hb : (j + 1) * hb]
        old_sums.append(jnp.sum(jnp.transpose(folded), axis=0, keepdims=True))
    old_out = wo_ref[pl.ds(pl.multiple_of(quarter * hb + plane * rb, rb), rb), :].astype(F32)

    def pre(span):
        both = jnp.dot(kbuf[span, :], wcat[...], preferred_element_type=F32)
        return both[:, 0:hb], both[:, hb : 2 * hb]

    def grads(span, gate_pre, up_pre):
        back = lax.dot_general(sbuf[span, :], wback[...], NT, preferred_element_type=F32)
        sigma = jax.nn.sigmoid(gate_pre)
        swish = gate_pre * sigma
        act = (swish * up_pre).astype(BF16)
        d_gate = (back * up_pre * (sigma * (1.0 + gate_pre * (1.0 - sigma)))).astype(BF16)
        d_up = (back * swish).astype(BF16)
        both = jnp.concatenate([d_gate, d_up], axis=1)
        g_in = lax.dot_general(both, kbuf[span, :], TN, preferred_element_type=F32)
        g_out = lax.dot_general(act, sbuf[span, :], TN, preferred_element_type=F32)
        return g_in, g_out

    k_mate.wait_recv()
    s_mate.wait_recv()
    first = slice(0, 2 * tokens)
    gate_pre, up_pre = pre(first)
    g_in, g_out = grads(first, gate_pre, up_pre)
    acc_in[...] = g_in
    acc_out[...] = g_out

    second = slice(2 * tokens, 4 * tokens)
    k_across.wait_recv()
    k_forward = token_copy(kbuf, 0, 2, 3, mate)
    k_forward.wait_recv()
    gate_pre, up_pre = pre(second)
    s_across.wait_recv()
    s_forward = token_copy(sbuf, 1, 2, 3, mate)
    q_copy = send(q_ref, qbuf.at[rows(1)], q_send, q_recv, across)
    s_forward.wait_recv()
    g_in, g_out = grads(second, gate_pre, up_pre)
    acc_in[...] += g_in
    acc_out[...] += g_out

    def part(p):
        top = acc_in[:, pl.ds(pl.multiple_of(p * db, db), db)]
        low = acc_out[pl.ds(pl.multiple_of(p * rb, rb), rb), :]
        return top, low

    g_copies = {}
    for d in (2, 1, 3) if planes == 4 else range(1, planes):
        top, low = part(plane_at(d))
        gsend[d - 1, 0 : 2 * hb, :] = top.astype(BF16)
        for j in range(spread):
            gsend[d - 1, 2 * hb + j * rb : 2 * hb + (j + 1) * rb, :] = low[
                :, j * db : (j + 1) * db
            ].astype(BF16)
        slot = planes - 1 - d
        g_copies[d] = send(
            gsend.at[d - 1], grecv.at[slot], g_send.at[d - 1], g_recv.at[slot], same_spot(d)
        )
    qbuf[rows(0), :] = q_ref[...]
    top, low = part(plane)
    sum_top = old[...] + top
    sum_low = [
        old_out[:, j * db : (j + 1) * db] + low[:, j * db : (j + 1) * db] for j in range(spread)
    ]
    for slot in range(planes - 1):
        g_copies[planes - 1 - slot].wait_recv()
        sum_top = sum_top + grecv[slot, 0 : 2 * hb, :].astype(F32)
        for j in range(spread):
            sum_low[j] = sum_low[j] + grecv[
                slot, 2 * hb + j * rb : 2 * hb + (j + 1) * rb, :
            ].astype(F32)

    squares = sum_top * sum_top
    mine = [
        jnp.sum(squares[i * hb : (i + 1) * hb, :], axis=0, keepdims=True) for i in range(2)
    ]
    stat[0] = jnp.concatenate([jnp.broadcast_to(one, (4, db)) for one in mine], axis=0)
    st_copies = [
        send(stat.at[0], stat.at[i + 1], st_send.at[i], st_recv.at[i], peer)
        for i, peer in enumerate((mate, across, diagonal))
    ]

    new_sum = sum(jnp.sum(one * one, axis=1, keepdims=True) for one in sum_low)
    old_sum = jnp.sum(old_out * old_out, axis=1, keepdims=True)
    factor = jnp.sqrt(old_sum / width + epsilon) / jnp.sqrt(new_sum / width + epsilon)
    wbuf[0, plane, 0 : 2 * hb, :] = sum_top.astype(BF16)
    for j in range(spread):
        wbuf[0, plane, 2 * hb + j * rb : 2 * hb + (j + 1) * rb, :] = (
            sum_low[j] * factor
        ).astype(BF16)

    w_copies = {}
    for d in (2, 1, 3) if planes == 4 else range(1, planes):
        slot = planes - 1 - d
        w_copies[d] = send(
            wbuf.at[0, plane], wbuf.at[0, plane], w_send.at[d - 1], w_recv.at[slot], same_spot(d)
        )

    def to_mate(index, p):
        return send(wbuf.at[0, p], wbuf.at[1, p], c_send.at[index], c_recv.at[index], mate)

    c_copies = [to_mate(0, plane)]

    for copy in st_copies:
        copy.wait_recv()
    total = stat[0] + stat[1] + stat[2] + stat[3]
    olds = jnp.concatenate([jnp.broadcast_to(one, (4, db)) for one in old_sums], axis=0)
    fact[plane] = jnp.sqrt(olds / hidden + epsilon) / jnp.sqrt(total / hidden + epsilon)
    f_copies = {}
    for d in range(1, planes):
        slot = planes - 1 - d
        f_copies[d] = send(
            fact.at[plane], fact.at[plane], f_send.at[d - 1], f_recv.at[slot], same_spot(d)
        )

    def arrived(buf, recv_sem, peer, send_sem):
        pltpu.make_async_remote_copy(
            src_ref=buf,
            dst_ref=buf,
            send_sem=send_sem,
            recv_sem=recv_sem,
            device_id=peer,
            device_id_type=MESH,
        ).wait_recv()

    def place(which, p):
        to = pl.ds(pl.multiple_of(p * db, db), db)
        for i in range(2):
            rows_of = slice(i * hb, (i + 1) * hb)
            scaled = wbuf[which, p, rows_of, :].astype(F32) * fact[p, 4 * i : 4 * i + 1, :]
            wq[which * 2 * hb + i * hb : which * 2 * hb + (i + 1) * hb, to] = scaled.astype(BF16)
        for j in range(spread):
            wo[pl.ds(pl.multiple_of(which * hb + p * rb, rb), rb), j * db : (j + 1) * db] = wbuf[
                which, p, 2 * hb + j * rb : 2 * hb + (j + 1) * rb, :
            ]

    place(0, plane)
    arrived(wbuf.at[1, plane], c_recv.at[0], mate, c_send.at[0])
    place(1, plane)
    order = (1, 3, 2) if planes == 4 else tuple(range(1, planes))
    for d in order:
        p = plane_at(d)
        arrived(wbuf.at[0, p], w_recv.at[d - 1], same_spot(d), w_send.at[d - 1])
        c_copies.append(to_mate(d, p))
        arrived(fact.at[p], f_recv.at[d - 1], same_spot(d), f_send.at[d - 1])
        place(0, p)
    q_copy.wait_recv()
    for d in order:
        p = plane_at(d)
        arrived(wbuf.at[1, p], c_recv.at[d], mate, c_send.at[d])
        place(1, p)

    def apply(span):
        pres = lax.dot_general(qbuf[span, :], wq[...], NT, preferred_element_type=F32)
        acts = []
        for which in range(2):
            gate = pres[:, which * 2 * hb : which * 2 * hb + hb]
            up = pres[:, which * 2 * hb + hb : (which + 1) * 2 * hb]
            acts.append((gate * jax.nn.sigmoid(gate) * up).astype(BF16))
        return jnp.dot(jnp.concatenate(acts, axis=1), wo[...], preferred_element_type=F32)

    psend[...] = apply(slice(tokens, 2 * tokens)).astype(BF16)
    p_copy = send(psend, precv, p_send, p_recv, across)
    own = apply(slice(0, tokens))
    p_copy.wait_recv()
    o_ref[...] = (own + precv[...].astype(F32)).astype(BF16)

    outgoing = [k_across, s_across, k_mate, s_mate, k_forward, s_forward, q_copy, p_copy]
    outgoing += list(g_copies.values()) + list(w_copies.values()) + list(f_copies.values())
    outgoing += st_copies + c_copies
    for copy in outgoing:
        copy.wait_send()


def fused(keys, values, queries, learn_rate, w_gate, w_up, w_out):
    tokens, width = keys.shape
    hidden = w_gate.shape[1]
    planes = lax.axis_size("seq") // 2
    hb, db = hidden // 4, width // planes
    part_rows = 3 * hb
    vmem = pltpu.VMEM
    dma = pltpu.SemaphoreType.DMA
    scratch = [
        vmem((4 * tokens, width), BF16),
        vmem((4 * tokens, width), BF16),
        vmem((2 * tokens, width), BF16),
        vmem((width, 2 * hb), BF16),
        vmem((hb, width), BF16),
        vmem((2 * hb, db), F32),
        vmem((2 * hb, width), F32),
        vmem((hb, width), F32),
        vmem((planes - 1, part_rows, db), BF16),
        vmem((planes - 1, part_rows, db), BF16),
        vmem((4, 8, db), F32),
        vmem((planes, 8, db), F32),
        vmem((2, planes, part_rows, db), BF16),
        vmem((4 * hb, width), BF16),
        vmem((2 * hb, width), BF16),
        vmem((tokens, width), BF16),
        vmem((tokens, width), BF16),
        dma((2, 3)),
        dma((2, 3)),
        dma,
        dma,
        dma((planes - 1,)),
        dma((planes - 1,)),
        dma((3,)),
        dma((3,)),
        dma((planes - 1,)),
        dma((planes - 1,)),
        dma((planes - 1,)),
        dma((planes - 1,)),
        dma((planes,)),
        dma((planes,)),
        dma,
        dma,
    ]
    return pl.pallas_call(
        functools.partial(kernel, planes),
        out_shape=jax.ShapeDtypeStruct((tokens, width), BF16),
        in_specs=[pl.BlockSpec(memory_space=pltpu.VMEM)] * 7,
        out_specs=pl.BlockSpec(memory_space=pltpu.VMEM),
        scratch_shapes=scratch,
        compiler_params=pltpu.CompilerParams(
            collective_id=0, has_side_effects=True, vmem_limit_bytes=40 * 2**20
        ),
        cost_estimate=pl.CostEstimate(
            flops=2 * tokens * width * hidden * 9, bytes_accessed=2 * 2**20, transcendentals=0
        ),
    )(learn_rate.reshape(1, tokens), keys, values, queries, w_gate, w_up, w_out)


def renorm(weight, grads):
    old = weight.astype(F32)
    update = old + grads
    factor = jnp.sqrt(jnp.mean(old * old, axis=1, keepdims=True) + epsilon) / jnp.sqrt(
        jnp.mean(update * update, axis=1, keepdims=True) + epsilon
    )
    return (update * factor).astype(BF16)


def plain(keys, values, queries, learn_rate, w_gate, w_up, w_out):
    hidden = w_gate.shape[1]
    axes = ("seq", "outer")
    shards = lax.axis_size(axes)
    rows_in, rows_out = w_gate.shape[0] // shards, w_out.shape[0] // shards
    position = lax.axis_index(axes)
    scaled = (learn_rate[:, None] * values.astype(F32)).astype(BF16)
    gate_pre = jnp.dot(keys, w_gate, preferred_element_type=F32)
    up_pre = jnp.dot(keys, w_up, preferred_element_type=F32)
    back = lax.dot_general(scaled, w_out, NT, preferred_element_type=F32)
    activation = (jax.nn.silu(gate_pre) * up_pre).astype(BF16)
    d_gate = (back * up_pre * silu_grad(gate_pre)).astype(BF16)
    d_up = (back * jax.nn.silu(gate_pre)).astype(BF16)
    both = jnp.concatenate([d_gate, d_up], axis=1)
    full_in = lax.dot_general(keys, both, TN, preferred_element_type=F32)
    full_out = lax.dot_general(activation, scaled, TN, preferred_element_type=F32)
    grad_in = lax.psum_scatter(full_in, axes, scatter_dimension=0, tiled=True)
    grad_out = lax.psum_scatter(full_out, axes, scatter_dimension=0, tiled=True)
    own_gate = lax.dynamic_slice_in_dim(w_gate, position * rows_in, rows_in, 0)
    own_up = lax.dynamic_slice_in_dim(w_up, position * rows_in, rows_in, 0)
    own_out = lax.dynamic_slice_in_dim(w_out, position * rows_out, rows_out, 0)
    news = (
        renorm(own_gate, grad_in[:, :hidden]),
        renorm(own_up, grad_in[:, hidden:]),
        renorm(own_out, grad_out),
    )
    gate, up, out = [lax.all_gather(new, axes, axis=0, tiled=True) for new in news]
    q_gate = jnp.dot(queries, gate, preferred_element_type=F32)
    q_up = jnp.dot(queries, up, preferred_element_type=F32)
    q_act = (jax.nn.silu(q_gate) * q_up).astype(BF16)
    return jnp.dot(q_act, out, preferred_element_type=F32).astype(BF16)


def local(keys, values, queries, learn_rate, w_gate, w_up, w_out):
    width, hidden = w_gate.shape
    tokens = keys.shape[0]
    seq, cores = lax.axis_size("seq"), lax.axis_size("outer")
    planes = seq // 2
    fits = (
        cores == 2
        and seq % 2 == 0
        and planes > 1
        and width % (128 * planes) == 0
        and hidden % (4 * 32 * planes) == 0
        and hidden // 4 == 128
        and tokens == 128
    )
    chosen = fused if fits else plain
    return chosen(keys, values, queries, learn_rate, w_gate, w_up, w_out)


def solution(mesh):
    placed = (
        P(("grp", "seq", "outer"), None),
        P(("grp", "seq", "outer"), None),
        P(("grp", "seq", "outer"), None),
        P(("grp", "seq", "outer")),
        P("grp", None),
        P("grp", None),
        P("grp", None),
    )
    return jax.shard_map(
        local,
        mesh=mesh,
        in_specs=placed,
        out_specs=P(("grp", "seq", "outer"), None),
        check_vma=False,
    )
```

time: 188 us -> 47.8 us (0.25)
  waiting for transfers between devices: 99.9 us -> 0 us
  blocking collectives: 60.6 us -> 0 us
  Pallas kernels: 0 us -> 40.3 us
  between operations: 13.5 us -> 0.02 us
  matrix products: 7.17 us -> 0 us
  local copies, waits for them, and re-layouts: 2.78 us -> 7.15 us
  other arithmetic: 3.95 us -> 0 us
    reduce_scatter x2 -> x0, waiting for transfers between devices: 99.8 us -> none  [the longest x1 57.8 us: local(): lax.psum_scatter(full_out, ('seq', 'outer'), scatter_dimension=0, tiled=T...]
    all_gather x3 -> x0, blocking collectives: 60.6 us -> none  [the longest x1 20.9 us: local(): lax.all_gather(new_out, ('seq', 'outer'), axis=0, tiled=True)]
    pallas_call x0 -> x1, Pallas kernels: none -> 40.3 us  [fused(): pl.pallas_call(functools.partial(kernel, planes), out_shape=jax.ShapeDtyp...]
    dot_general x7 -> x0, matrix products: 7.17 us -> none  [the longest x1 1.43 us: local(): lax.dot_general(scaled, w_out, contract_last, preferred_element_type=jnp....]
    unnamed x9 -> x15, local copies, waits for them, and re-layouts: 2.78 us -> 7.15 us
    reduce_sum x2 -> x0, other arithmetic: 2.04 us -> none  [renorm(): jnp.mean(old * old, axis=1, keepdims=True) + epsilon]
    convert_element_type x2 -> x0, other arithmetic: 1.89 us -> none  [renorm(): return (update * factor).astype(jnp.bfloat16)]
  transfers between devices with their start and end apart: 2 -> 0, of which waited for: 2 -> 0; matrix products, arithmetic and copies ran while one was open for 2% -> 0% of each run, Pallas kernels for 0% -> 0%
where the time goes in v1:
time: 47.8 us; the launch traced here: 47.5 us
  Pallas kernels  40.3 us (84%)
  local copies, waits for them, and re-layouts  7.15 us (15%)
    pallas_call x1, Pallas kernels, fused(): pl.pallas_call(functools.partial(kernel, planes), out_shape=jax.ShapeDtyp...  40.3 us
    unnamed x15, local copies, waits for them, and re-layouts  7.15 us

profile of v1, /device:TPU:0, one launch (start us, length us, event | category | flops | bytes accessed | tf_op | source)
XLA Modules:
  0.0 47.5 jit_solution(13520944565260558720)
XLA Ops:
  0.0 0.0 copy-start.6
  0.0 0.7 %copy-done.6 = f32[128]{0:T(128)S(1)} copy-done((f32[128]{0:T(128)S(1)}, f32[128]{0:T(128)}, u32[]{:S(2)}) %copy-start.6) | copy-done | bytes 536
  0.7 0.0 copy-start
  0.7 1.0 %copy-done = bf16[512,512]{1,0:T(8,128)(2,1)S(1)} copy-done((bf16[512,512]{1,0:T(8,128)(2,1)S(1)}, bf16[512,512]{1,0:T(8,128)(2,1)}, u32[]{:S(2)}) %copy-start) | copy-done | bytes 524312
  1.7 0.0 copy-start.1
  1.7 1.0 %copy-done.1 = bf16[512,512]{1,0:T(8,128)(2,1)S(1)} copy-done((bf16[512,512]{1,0:T(8,128)(2,1)S(1)}, bf16[512,512]{1,0:T(8,128)(2,1)}, u32[]{:S(2)}) %copy-start.1) | copy-done | bytes 524312
  2.7 0.0 copy-start.2
  2.7 1.0 %copy-done.2 = bf16[512,512]{1,0:T(8,128)(2,1)S(1)} copy-done((bf16[512,512]{1,0:T(8,128)(2,1)S(1)}, bf16[512,512]{1,0:T(8,128)(2,1)}, u32[]{:S(2)}) %copy-start.2) | copy-done | bytes 524312
  3.8 0.0 copy-start.3
  3.8 0.9 %copy-done.3 = bf16[128,512]{1,0:T(8,128)(2,1)S(1)} copy-done((bf16[128,512]{1,0:T(8,128)(2,1)S(1)}, bf16[128,512]{1,0:T(8,128)(2,1)}, u32[]{:S(2)}) %copy-start.3) | copy-done | bytes 131096
  4.7 0.0 copy-start.4
  4.7 0.9 %copy-done.4 = bf16[128,512]{1,0:T(8,128)(2,1)S(1)} copy-done((bf16[128,512]{1,0:T(8,128)(2,1)S(1)}, bf16[128,512]{1,0:T(8,128)(2,1)}, u32[]{:S(2)}) %copy-start.4) | copy-done | bytes 131096
  5.6 0.0 copy-start.5
  5.6 0.9 %copy-done.5 = bf16[128,512]{1,0:T(8,128)(2,1)S(1)} copy-done((bf16[128,512]{1,0:T(8,128)(2,1)S(1)}, bf16[128,512]{1,0:T(8,128)(2,1)}, u32[]{:S(2)}) %copy-start.5) | copy-done | bytes 131096
  6.5 40.3 %shard_map.73 = bf16[128,512]{1,0:T(8,128)(2,1)S(1)} custom-call(f32[1,128]{1,0:T(1,128)S(1)} %bitcast.1, bf16[128,512]{1,0:T(8,128)(2,1)S(1)} %copy-done.3, bf16[128,512]{1,0:T(8,128)(2,1)S(1)} %copy-done.4, bf16[128,512]{1,0:T(8,128)(2,1)S(1)} %copy-done.5, bf16[512,512]{1,0:T(8,128)(2,1)S(1)} %copy-done, bf16[512,512]{1,0:T(8,128)(2,1)S(1)} %copy-done.1, ...), custom_call_target="tpu_custom_call" | custom-call | flops 603979776 | bytes 2097152 | tf_op jit(solution)/shard_map/pallas_call | solution.py:358
  46.8 0.7 %copy.9 = bf16[128,512]{1,0:T(8,128)(2,1)} copy(bf16[128,512]{1,0:T(8,128)(2,1)S(1)} %shard_map.73) | data formatting | bytes 262144
Async XLA Ops:
  0.0 0.7 %copy-start.6 = (f32[128]{0:T(128)S(1)}, f32[128]{0:T(128)}, u32[]{:S(2)}) copy-start(f32[128]{0:T(128)} %param.10) | copy-start | bytes 1540
  0.7 1.0 %copy-start = (bf16[512,512]{1,0:T(8,128)(2,1)S(1)}, bf16[512,512]{1,0:T(8,128)(2,1)}, u32[]{:S(2)}) copy-start(bf16[512,512]{1,0:T(8,128)(2,1)} %wg_ref.1) | copy-start | bytes 1572868
  1.7 1.0 %copy-start.1 = (bf16[512,512]{1,0:T(8,128)(2,1)S(1)}, bf16[512,512]{1,0:T(8,128)(2,1)}, u32[]{:S(2)}) copy-start(bf16[512,512]{1,0:T(8,128)(2,1)} %wu_ref.1) | copy-start | bytes 1572868
  2.7 1.0 %copy-start.2 = (bf16[512,512]{1,0:T(8,128)(2,1)S(1)}, bf16[512,512]{1,0:T(8,128)(2,1)}, u32[]{:S(2)}) copy-start(bf16[512,512]{1,0:T(8,128)(2,1)} %wo_ref.1) | copy-start | bytes 1572868
  3.8 0.9 %copy-start.3 = (bf16[128,512]{1,0:T(8,128)(2,1)S(1)}, bf16[128,512]{1,0:T(8,128)(2,1)}, u32[]{:S(2)}) copy-start(bf16[128,512]{1,0:T(8,128)(2,1)} %k_ref.1) | copy-start | bytes 393220
  4.7 0.9 %copy-start.4 = (bf16[128,512]{1,0:T(8,128)(2,1)S(1)}, bf16[128,512]{1,0:T(8,128)(2,1)}, u32[]{:S(2)}) copy-start(bf16[128,512]{1,0:T(8,128)(2,1)} %v_ref.1) | copy-start | bytes 393220
  5.6 0.9 %copy-start.5 = (bf16[128,512]{1,0:T(8,128)(2,1)S(1)}, bf16[128,512]{1,0:T(8,128)(2,1)}, u32[]{:S(2)}) copy-start(bf16[128,512]{1,0:T(8,128)(2,1)} %q_ref.1) | copy-start | bytes 393220

commit v2 on v1

--- a/solution.py
+++ b/solution.py
@@ -35,6 +35,9 @@
     qbuf,
     wcat,
     wback,
+    vbuf,
+    lrbuf,
+    wrows,
     old,
     acc_in,
     acc_out,
@@ -63,6 +66,7 @@
     c_recv,
     p_send,
     p_recv,
+    load,
 ):
     tokens, width = k_ref.shape
     hidden = wg_ref.shape[1]
@@ -86,18 +90,35 @@
     def same_spot(distance):
         return {"seq": plane_at(distance) * 2 + side}
 
+    def rows(slot):
+        return pl.ds(slot * tokens, tokens)
+
+    my_cols = pl.ds(pl.multiple_of(plane * db, db), db)
+    moves = (
+        (lr_ref, lrbuf),
+        (v_ref, vbuf),
+        (k_ref, kbuf.at[rows(0)]),
+        (wg_ref.at[:, cols], wcat.at[:, 0:hb]),
+        (wu_ref.at[:, cols], wcat.at[:, hb : 2 * hb]),
+        (wo_ref.at[cols], wback),
+        (wg_ref.at[my_cols], wrows.at[0]),
+        (wu_ref.at[my_cols], wrows.at[1]),
+        (q_ref, qbuf.at[rows(0)]),
+    )
+    loads = [pltpu.make_async_copy(a, b, load.at[i]) for i, (a, b) in enumerate(moves)]
+    for copy in loads:
+        copy.start()
+
     barrier = pltpu.get_barrier_semaphore()
     peers = [mate, across, diagonal] + [same_spot(d) for d in range(1, planes)]
     for peer in peers:
         pl.semaphore_signal(barrier, inc=1, device_id=peer, device_id_type=MESH)
 
-    def rows(slot):
-        return pl.ds(slot * tokens, tokens)
-
-    lr_cols = jnp.transpose(jnp.broadcast_to(lr_ref[...], (tokens, tokens)))
+    loads[0].wait()
+    loads[1].wait()
+    lr_cols = jnp.transpose(jnp.broadcast_to(lrbuf[...], (tokens, tokens)))
     rate = lr_cols[:, 0:1]
-    sbuf[rows(0), :] = (rate * v_ref[...].astype(F32)).astype(BF16)
-    kbuf[rows(0), :] = k_ref[...]
+    sbuf[rows(0), :] = (rate * vbuf[...].astype(F32)).astype(BF16)
     pl.semaphore_wait(barrier, len(peers))
 
     def send(src, dst, send_sem, recv_sem, peer):
@@ -112,46 +133,45 @@
         copy.start()
         return copy
 
-    def token_copy(buf, kind, src_slot, dst_slot, peer):
+    def token_copy(src, buf, kind, dst_slot, peer):
         return send(
-            buf.at[rows(src_slot)],
+            src,
             buf.at[rows(dst_slot)],
             tok_send.at[kind, dst_slot - 1],
             tok_recv.at[kind, dst_slot - 1],
             peer,
         )
 
-    k_across = token_copy(kbuf, 0, 0, 2, across)
-    s_across = token_copy(sbuf, 1, 0, 2, across)
-    k_mate = token_copy(kbuf, 0, 0, 1, mate)
-    s_mate = token_copy(sbuf, 1, 0, 1, mate)
-
-    wcat[:, 0:hb] = wg_ref[:, cols]
-    wcat[:, hb : 2 * hb] = wu_ref[:, cols]
-    wback[...] = wo_ref[cols, :]
-
-    my_cols = pl.ds(pl.multiple_of(plane * db, db), db)
+    k_across = token_copy(k_ref, kbuf, 0, 2, across)
+    s_across = token_copy(sbuf.at[rows(0)], sbuf, 1, 2, across)
+    k_mate = token_copy(k_ref, kbuf, 0, 1, mate)
+    s_mate = token_copy(sbuf.at[rows(0)], sbuf, 1, 1, mate)
+    for copy in loads[2:]:
+        copy.wait()
+
     old_sums = []
-    for i, ref in enumerate((wg_ref, wu_ref)):
-        old[i * hb : (i + 1) * hb, :] = jnp.transpose(ref[my_cols, cols].astype(F32))
-        whole = ref[my_cols, :].astype(F32)
+    for i in range(2):
+        old[i * hb : (i + 1) * hb, :] = jnp.transpose(wrows[i, :, cols].astype(F32))
+        whole = wrows[i].astype(F32)
         squares = whole * whole
         folded = squares[:, 0:hb]
         for j in range(1, 4):
             folded = folded + squares[:, j * hb : (j + 1) * hb]
         old_sums.append(jnp.sum(jnp.transpose(folded), axis=0, keepdims=True))
-    old_out = wo_ref[pl.ds(pl.multiple_of(quarter * hb + plane * rb, rb), rb), :].astype(F32)
+    old_out = wback[pl.ds(pl.multiple_of(plane * rb, rb), rb), :].astype(F32)
 
     def pre(span):
         both = jnp.dot(kbuf[span, :], wcat[...], preferred_element_type=F32)
-        return both[:, 0:hb], both[:, hb : 2 * hb]
-
-    def grads(span, gate_pre, up_pre):
-        back = lax.dot_general(sbuf[span, :], wback[...], NT, preferred_element_type=F32)
+        gate_pre, up_pre = both[:, 0:hb], both[:, hb : 2 * hb]
         sigma = jax.nn.sigmoid(gate_pre)
         swish = gate_pre * sigma
         act = (swish * up_pre).astype(BF16)
-        d_gate = (back * up_pre * (sigma * (1.0 + gate_pre * (1.0 - sigma)))).astype(BF16)
+        slope = up_pre * (sigma * (1.0 + gate_pre * (1.0 - sigma)))
+        return act, swish, slope
+
+    def grads(span, act, swish, slope):
+        back = lax.dot_general(sbuf[span, :], wback[...], NT, preferred_element_type=F32)
+        d_gate = (back * slope).astype(BF16)
         d_up = (back * swish).astype(BF16)
         both = jnp.concatenate([d_gate, d_up], axis=1)
         g_in = lax.dot_general(both, kbuf[span, :], TN, preferred_element_type=F32)
@@ -161,21 +181,20 @@
     k_mate.wait_recv()
     s_mate.wait_recv()
     first = slice(0, 2 * tokens)
-    gate_pre, up_pre = pre(first)
-    g_in, g_out = grads(first, gate_pre, up_pre)
+    g_in, g_out = grads(first, *pre(first))
     acc_in[...] = g_in
     acc_out[...] = g_out
 
     second = slice(2 * tokens, 4 * tokens)
     k_across.wait_recv()
-    k_forward = token_copy(kbuf, 0, 2, 3, mate)
+    k_forward = token_copy(kbuf.at[rows(2)], kbuf, 0, 3, mate)
     k_forward.wait_recv()
-    gate_pre, up_pre = pre(second)
+    ready = pre(second)
     s_across.wait_recv()
-    s_forward = token_copy(sbuf, 1, 2, 3, mate)
+    s_forward = token_copy(sbuf.at[rows(2)], sbuf, 1, 3, mate)
     q_copy = send(q_ref, qbuf.at[rows(1)], q_send, q_recv, across)
     s_forward.wait_recv()
-    g_in, g_out = grads(second, gate_pre, up_pre)
+    g_in, g_out = grads(second, *ready)
     acc_in[...] += g_in
     acc_out[...] += g_out
 
@@ -196,7 +215,6 @@
         g_copies[d] = send(
             gsend.at[d - 1], grecv.at[slot], g_send.at[d - 1], g_recv.at[slot], same_spot(d)
         )
-    qbuf[rows(0), :] = q_ref[...]
     top, low = part(plane)
     sum_top = old[...] + top
     sum_low = [
@@ -326,6 +344,9 @@
         vmem((2 * tokens, width), BF16),
         vmem((width, 2 * hb), BF16),
         vmem((hb, width), BF16),
+        vmem((tokens, width), BF16),
+        vmem((1, tokens), F32),
+        vmem((2, db, hidden), BF16),
         vmem((2 * hb, db), F32),
         vmem((2 * hb, width), F32),
         vmem((hb, width), F32),
@@ -354,11 +375,12 @@
         dma((planes,)),
         dma,
         dma,
+        dma((9,)),
     ]
     return pl.pallas_call(
         functools.partial(kernel, planes),
         out_shape=jax.ShapeDtypeStruct((tokens, width), BF16),
-        in_specs=[pl.BlockSpec(memory_space=pltpu.VMEM)] * 7,
+        in_specs=[pl.BlockSpec(memory_space=pltpu.HBM)] * 7,
         out_specs=pl.BlockSpec(memory_space=pltpu.VMEM),
         scratch_shapes=scratch,
         compiler_params=pltpu.CompilerParams(

time: 47.8 us -> 48.9 us (1.023)
  Pallas kernels: 40.3 us -> 41.5 us
    pallas_call x1, Pallas kernels: 40.3 us -> 41.5 us  [fused(): pl.pallas_call(functools.partial(kernel, planes), out_shape=jax.ShapeDtyp...]
where the time goes in v2:
time: 48.9 us; the launch traced here: 48.6 us
  Pallas kernels  41.5 us (85%)
  local copies, waits for them, and re-layouts  7.15 us (15%)
    pallas_call x1, Pallas kernels, fused(): pl.pallas_call(functools.partial(kernel, planes), out_shape=jax.ShapeDtyp...  41.5 us
    unnamed x15, local copies, waits for them, and re-layouts  7.15 us

profile of v2, /device:TPU:0, one launch (start us, length us, event | category | flops | bytes accessed | tf_op | source)
XLA Modules:
  0.0 48.6 jit_solution(587917881956909022)
XLA Ops:
  0.0 0.0 copy-start.6
  0.0 0.7 %copy-done.6 = f32[128]{0:T(128)S(1)} copy-done((f32[128]{0:T(128)S(1)}, f32[128]{0:T(128)}, u32[]{:S(2)}) %copy-start.6) | copy-done | bytes 536
  0.7 0.0 copy-start
  0.7 1.0 %copy-done = bf16[512,512]{1,0:T(8,128)(2,1)S(1)} copy-done((bf16[512,512]{1,0:T(8,128)(2,1)S(1)}, bf16[512,512]{1,0:T(8,128)(2,1)}, u32[]{:S(2)}) %copy-start) | copy-done | bytes 524312
  1.7 0.0 copy-start.1
  1.7 1.0 %copy-done.1 = bf16[512,512]{1,0:T(8,128)(2,1)S(1)} copy-done((bf16[512,512]{1,0:T(8,128)(2,1)S(1)}, bf16[512,512]{1,0:T(8,128)(2,1)}, u32[]{:S(2)}) %copy-start.1) | copy-done | bytes 524312
  2.7 0.0 copy-start.2
  2.7 1.0 %copy-done.2 = bf16[512,512]{1,0:T(8,128)(2,1)S(1)} copy-done((bf16[512,512]{1,0:T(8,128)(2,1)S(1)}, bf16[512,512]{1,0:T(8,128)(2,1)}, u32[]{:S(2)}) %copy-start.2) | copy-done | bytes 524312
  3.8 0.0 copy-start.3
  3.8 0.9 %copy-done.3 = bf16[128,512]{1,0:T(8,128)(2,1)S(1)} copy-done((bf16[128,512]{1,0:T(8,128)(2,1)S(1)}, bf16[128,512]{1,0:T(8,128)(2,1)}, u32[]{:S(2)}) %copy-start.3) | copy-done | bytes 131096
  4.7 0.0 copy-start.4
  4.7 0.9 %copy-done.4 = bf16[128,512]{1,0:T(8,128)(2,1)S(1)} copy-done((bf16[128,512]{1,0:T(8,128)(2,1)S(1)}, bf16[128,512]{1,0:T(8,128)(2,1)}, u32[]{:S(2)}) %copy-start.4) | copy-done | bytes 131096
  5.6 0.0 copy-start.5
  5.6 0.9 %copy-done.5 = bf16[128,512]{1,0:T(8,128)(2,1)S(1)} copy-done((bf16[128,512]{1,0:T(8,128)(2,1)S(1)}, bf16[128,512]{1,0:T(8,128)(2,1)}, u32[]{:S(2)}) %copy-start.5) | copy-done | bytes 131096
  6.5 41.5 %shard_map.73 = bf16[128,512]{1,0:T(8,128)(2,1)S(1)} custom-call(f32[1,128]{1,0:T(1,128)S(1)} %bitcast.1, bf16[128,512]{1,0:T(8,128)(2,1)S(1)} %copy-done.3, bf16[128,512]{1,0:T(8,128)(2,1)S(1)} %copy-done.4, bf16[128,512]{1,0:T(8,128)(2,1)S(1)} %copy-done.5, bf16[512,512]{1,0:T(8,128)(2,1)S(1)} %copy-done, bf16[512,512]{1,0:T(8,128)(2,1)S(1)} %copy-done.1, ...), custom_call_target="tpu_custom_call" | custom-call | flops 603979776 | bytes 2097152 | tf_op jit(solution)/shard_map/pallas_call | solution.py:380
  48.0 0.7 %copy.9 = bf16[128,512]{1,0:T(8,128)(2,1)} copy(bf16[128,512]{1,0:T(8,128)(2,1)S(1)} %shard_map.73) | data formatting | bytes 262144
Async XLA Ops:
  0.0 0.7 %copy-start.6 = (f32[128]{0:T(128)S(1)}, f32[128]{0:T(128)}, u32[]{:S(2)}) copy-start(f32[128]{0:T(128)} %param.10) | copy-start | bytes 1540
  0.7 1.0 %copy-start = (bf16[512,512]{1,0:T(8,128)(2,1)S(1)}, bf16[512,512]{1,0:T(8,128)(2,1)}, u32[]{:S(2)}) copy-start(bf16[512,512]{1,0:T(8,128)(2,1)} %wg_ref.1) | copy-start | bytes 1572868
  1.7 1.0 %copy-start.1 = (bf16[512,512]{1,0:T(8,128)(2,1)S(1)}, bf16[512,512]{1,0:T(8,128)(2,1)}, u32[]{:S(2)}) copy-start(bf16[512,512]{1,0:T(8,128)(2,1)} %wu_ref.1) | copy-start | bytes 1572868
  2.7 1.0 %copy-start.2 = (bf16[512,512]{1,0:T(8,128)(2,1)S(1)}, bf16[512,512]{1,0:T(8,128)(2,1)}, u32[]{:S(2)}) copy-start(bf16[512,512]{1,0:T(8,128)(2,1)} %wo_ref.1) | copy-start | bytes 1572868
  3.8 0.9 %copy-start.3 = (bf16[128,512]{1,0:T(8,128)(2,1)S(1)}, bf16[128,512]{1,0:T(8,128)(2,1)}, u32[]{:S(2)}) copy-start(bf16[128,512]{1,0:T(8,128)(2,1)} %k_ref.1) | copy-start | bytes 393220
  4.7 0.9 %copy-start.4 = (bf16[128,512]{1,0:T(8,128)(2,1)S(1)}, bf16[128,512]{1,0:T(8,128)(2,1)}, u32[]{:S(2)}) copy-start(bf16[128,512]{1,0:T(8,128)(2,1)} %v_ref.1) | copy-start | bytes 393220
  5.6 0.9 %copy-start.5 = (bf16[128,512]{1,0:T(8,128)(2,1)S(1)}, bf16[128,512]{1,0:T(8,128)(2,1)}, u32[]{:S(2)}) copy-start(bf16[128,512]{1,0:T(8,128)(2,1)} %q_ref.1) | copy-start | bytes 393220

commit v3 on v2

--- a/solution.py
+++ b/solution.py
@@ -384,7 +384,7 @@
         out_specs=pl.BlockSpec(memory_space=pltpu.VMEM),
         scratch_shapes=scratch,
         compiler_params=pltpu.CompilerParams(
-            collective_id=0, has_side_effects=True, vmem_limit_bytes=40 * 2**20
+            collective_id=0, has_side_effects=True, vmem_limit_bytes=60 * 2**20
         ),
         cost_estimate=pl.CostEstimate(
             flops=2 * tokens * width * hidden * 9, bytes_accessed=2 * 2**20, transcendentals=0

time: 48.9 us -> 43 us (0.88)
  local copies, waits for them, and re-layouts: 7.15 us -> 1.57 us
    unnamed x15 -> x1, local copies, waits for them, and re-layouts: 7.15 us -> 1.57 us
where the time goes in v3:
time: 43 us; the launch traced here: 42.8 us
  Pallas kernels  41.3 us (96%)
  local copies, waits for them, and re-layouts  1.57 us (4%)
    pallas_call x1, Pallas kernels, fused(): pl.pallas_call(functools.partial(kernel, planes), out_shape=jax.ShapeDtyp...  41.3 us
    unnamed x1, local copies, waits for them, and re-layouts  1.57 us

profile of v3, /device:TPU:0, one launch (start us, length us, event | category | flops | bytes accessed | tf_op | source)
XLA Modules:
  0.0 42.8 jit_solution(5876163245182266330)
XLA Ops:
  0.0 41.3 %shard_map.73 = bf16[128,512]{1,0:T(8,128)(2,1)} custom-call(f32[1,128]{1,0:T(1,128)} %bitcast.1, bf16[128,512]{1,0:T(8,128)(2,1)} %k_ref.1, bf16[128,512]{1,0:T(8,128)(2,1)} %v_ref.1, bf16[128,512]{1,0:T(8,128)(2,1)} %q_ref.1, bf16[512,512]{1,0:T(8,128)(2,1)} %wg_ref.1, bf16[512,512]{1,0:T(8,128)(2,1)} %wu_ref.1, bf16[512,512]{1,0:T(8,128)(2,1)} %wo_ref.1), custom_call_target="tpu_custom_call" | custom-call | flops 603979776 | bytes 2097152 | tf_op jit(solution)/shard_map/pallas_call | solution.py:380
  41.3 1.6 %copy.9 = bf16[128,512]{1,0:T(8,128)(2,1)} copy(bf16[128,512]{1,0:T(8,128)(2,1)} %shard_map.73) | data formatting | bytes 262144

commit v4 on v3

--- a/solution.py
+++ b/solution.py
@@ -39,6 +39,7 @@
     lrbuf,
     wrows,
     old,
+    update,
     acc_in,
     acc_out,
     gsend,
@@ -80,6 +81,13 @@
     quarter = side * 2 + core
     cols = pl.ds(pl.multiple_of(quarter * hb, hb), hb)
 
+    inner = jnp.logical_or(plane == 1, plane == 2)
+    outer = jnp.logical_not(inner)
+    low_half = plane < 2
+    buddy = jnp.where(low_half, 1 - plane, 5 - plane)
+    fin = jnp.where(low_half, 2, 1)
+    far = jnp.where(low_half, 3, 0)
+
     mate = {"outer": 1 - core}
     across = {"seq": plane * 2 + 1 - side}
     diagonal = {"seq": plane * 2 + 1 - side, "outer": 1 - core}
@@ -133,6 +141,16 @@
         copy.start()
         return copy
 
+    def arrived(buf, recv_sem, peer, send_sem):
+        pltpu.make_async_remote_copy(
+            src_ref=buf,
+            dst_ref=buf,
+            send_sem=send_sem,
+            recv_sem=recv_sem,
+            device_id=peer,
+            device_id_type=MESH,
+        ).wait_recv()
+
     def token_copy(src, buf, kind, dst_slot, peer):
         return send(
             src,
@@ -159,6 +177,8 @@
             folded = folded + squares[:, j * hb : (j + 1) * hb]
         old_sums.append(jnp.sum(jnp.transpose(folded), axis=0, keepdims=True))
     old_out = wback[pl.ds(pl.multiple_of(plane * rb, rb), rb), :].astype(F32)
+    for j in range(spread):
+        old[2 * hb + j * rb : 2 * hb + (j + 1) * rb, :] = old_out[:, j * db : (j + 1) * db]
 
     def pre(span):
         both = jnp.dot(kbuf[span, :], wcat[...], preferred_element_type=F32)
@@ -185,48 +205,69 @@
     acc_in[...] = g_in
     acc_out[...] = g_out
 
-    second = slice(2 * tokens, 4 * tokens)
     k_across.wait_recv()
     k_forward = token_copy(kbuf.at[rows(2)], kbuf, 0, 3, mate)
+    ready = pre(rows(2))
     k_forward.wait_recv()
-    ready = pre(second)
+    last = pre(rows(3))
     s_across.wait_recv()
     s_forward = token_copy(sbuf.at[rows(2)], sbuf, 1, 3, mate)
     q_copy = send(q_ref, qbuf.at[rows(1)], q_send, q_recv, across)
-    s_forward.wait_recv()
-    g_in, g_out = grads(second, *ready)
+    g_in, g_out = grads(rows(2), *ready)
     acc_in[...] += g_in
     acc_out[...] += g_out
+    s_forward.wait_recv()
+    g_in, g_out = grads(rows(3), *last)
+    acc_in[...] += g_in
+    acc_out[...] += g_out
 
     def part(p):
-        top = acc_in[:, pl.ds(pl.multiple_of(p * db, db), db)]
-        low = acc_out[pl.ds(pl.multiple_of(p * rb, rb), rb), :]
-        return top, low
-
-    g_copies = {}
-    for d in (2, 1, 3) if planes == 4 else range(1, planes):
-        top, low = part(plane_at(d))
-        gsend[d - 1, 0 : 2 * hb, :] = top.astype(BF16)
-        for j in range(spread):
-            gsend[d - 1, 2 * hb + j * rb : 2 * hb + (j + 1) * rb, :] = low[
-                :, j * db : (j + 1) * db
-            ].astype(BF16)
-        slot = planes - 1 - d
-        g_copies[d] = send(
-            gsend.at[d - 1], grecv.at[slot], g_send.at[d - 1], g_recv.at[slot], same_spot(d)
+        return acc_in[:, pl.ds(pl.multiple_of(p * db, db), db)], acc_out[
+            pl.ds(pl.multiple_of(p * rb, rb), rb), :
+        ]
+
+    def stacked(p):
+        top, low = part(p)
+        return jnp.concatenate(
+            [top] + [low[:, j * db : (j + 1) * db] for j in range(spread)], axis=0
         )
-    top, low = part(plane)
-    sum_top = old[...] + top
-    sum_low = [
-        old_out[:, j * db : (j + 1) * db] + low[:, j * db : (j + 1) * db] for j in range(spread)
-    ]
-    for slot in range(planes - 1):
-        g_copies[planes - 1 - slot].wait_recv()
-        sum_top = sum_top + grecv[slot, 0 : 2 * hb, :].astype(F32)
-        for j in range(spread):
-            sum_low[j] = sum_low[j] + grecv[
-                slot, 2 * hb + j * rb : 2 * hb + (j + 1) * rb, :
-            ].astype(F32)
+
+    def g_copy(i, dst, slot):
+        return send(
+            gsend.at[i], grecv.at[slot], g_send.at[i], g_recv.at[slot], {"seq": dst * 2 + side}
+        )
+
+    def g_arrived(slot):
+        arrived(grecv.at[slot], g_recv.at[slot], mate, g_send.at[0])
+
+    gsend[0] = stacked(jnp.where(outer, far, fin)).astype(BF16)
+    g_copies = [g_copy(0, jnp.where(outer, buddy, fin), jnp.where(outer, 3, 0))]
+    gsend[1] = stacked(jnp.where(outer, fin, buddy)).astype(BF16)
+    g_copies.append(g_copy(1, jnp.where(outer, fin, buddy), jnp.where(outer, 1, 0)))
+
+    @pl.when(outer)
+    def _():
+        gsend[2] = stacked(buddy).astype(BF16)
+
+    @pl.when(inner)
+    def _():
+        g_arrived(3)
+        gsend[2] = (stacked(far) + grecv[3].astype(F32)).astype(BF16)
+
+    g_copies.append(g_copy(2, jnp.where(outer, buddy, far), jnp.where(outer, 2, 1)))
+    update[...] = old[...] + stacked(plane)
+    g_arrived(0)
+    update[...] += grecv[0].astype(F32)
+
+    @pl.when(inner)
+    def _():
+        g_arrived(2)
+        update[...] += grecv[2].astype(F32)
+
+    g_arrived(1)
+    update[...] += grecv[1].astype(F32)
+    sum_top = update[0 : 2 * hb, :]
+    sum_low = [update[2 * hb + j * rb : 2 * hb + (j + 1) * rb, :] for j in range(spread)]
 
     squares = sum_top * sum_top
     mine = [
@@ -247,12 +288,12 @@
             sum_low[j] * factor
         ).astype(BF16)
 
-    w_copies = {}
-    for d in (2, 1, 3) if planes == 4 else range(1, planes):
-        slot = planes - 1 - d
-        w_copies[d] = send(
-            wbuf.at[0, plane], wbuf.at[0, plane], w_send.at[d - 1], w_recv.at[slot], same_spot(d)
+    def w_copy(i, p, dst):
+        return send(
+            wbuf.at[0, p], wbuf.at[0, p], w_send.at[i], w_recv.at[p], {"seq": dst * 2 + side}
         )
+
+    w_copies = [w_copy(0, plane, jnp.where(outer, fin, buddy))]
 
     def to_mate(index, p):
         return send(wbuf.at[0, p], wbuf.at[1, p], c_send.at[index], c_recv.at[index], mate)
@@ -261,25 +302,20 @@
 
     for copy in st_copies:
         copy.wait_recv()
+    w_copies.append(w_copy(1, plane, jnp.where(outer, buddy, far)))
+
+    @pl.when(inner)
+    def _():
+        w_copy(2, plane, fin)
+
     total = stat[0] + stat[1] + stat[2] + stat[3]
     olds = jnp.concatenate([jnp.broadcast_to(one, (4, db)) for one in old_sums], axis=0)
     fact[plane] = jnp.sqrt(olds / hidden + epsilon) / jnp.sqrt(total / hidden + epsilon)
     f_copies = {}
     for d in range(1, planes):
-        slot = planes - 1 - d
         f_copies[d] = send(
-            fact.at[plane], fact.at[plane], f_send.at[d - 1], f_recv.at[slot], same_spot(d)
+            fact.at[plane], fact.at[plane], f_send.at[d - 1], f_recv.at[plane], same_spot(d)
         )
-
-    def arrived(buf, recv_sem, peer, send_sem):
-        pltpu.make_async_remote_copy(
-            src_ref=buf,
-            dst_ref=buf,
-            send_sem=send_sem,
-            recv_sem=recv_sem,
-            device_id=peer,
-            device_id_type=MESH,
-        ).wait_recv()
 
     def place(which, p):
         to = pl.ds(pl.multiple_of(p * db, db), db)
@@ -295,17 +331,25 @@
     place(0, plane)
     arrived(wbuf.at[1, plane], c_recv.at[0], mate, c_send.at[0])
     place(1, plane)
-    order = (1, 3, 2) if planes == 4 else tuple(range(1, planes))
-    for d in order:
-        p = plane_at(d)
-        arrived(wbuf.at[0, p], w_recv.at[d - 1], same_spot(d), w_send.at[d - 1])
-        c_copies.append(to_mate(d, p))
-        arrived(fact.at[p], f_recv.at[d - 1], same_spot(d), f_send.at[d - 1])
+    order = (
+        jnp.where(outer, buddy, far),
+        jnp.where(outer, fin, buddy),
+        jnp.where(outer, far, fin),
+    )
+    for i, p in enumerate(order):
+        arrived(wbuf.at[0, p], w_recv.at[p], mate, w_send.at[0])
+        c_copies.append(to_mate(i + 1, p))
+        if i == 0:
+
+            @pl.when(inner)
+            def _():
+                w_copy(3, far, buddy)
+
+        arrived(fact.at[p], f_recv.at[p], mate, f_send.at[0])
         place(0, p)
     q_copy.wait_recv()
-    for d in order:
-        p = plane_at(d)
-        arrived(wbuf.at[1, p], c_recv.at[d], mate, c_send.at[d])
+    for i, p in enumerate(order):
+        arrived(wbuf.at[1, p], c_recv.at[i + 1], mate, c_send.at[0])
         place(1, p)
 
     def apply(span):
@@ -324,10 +368,22 @@
     o_ref[...] = (own + precv[...].astype(F32)).astype(BF16)
 
     outgoing = [k_across, s_across, k_mate, s_mate, k_forward, s_forward, q_copy, p_copy]
-    outgoing += list(g_copies.values()) + list(w_copies.values()) + list(f_copies.values())
+    outgoing += g_copies + w_copies + list(f_copies.values())
     outgoing += st_copies + c_copies
     for copy in outgoing:
         copy.wait_send()
+
+    @pl.when(inner)
+    def _():
+        for i in (2, 3):
+            pltpu.make_async_remote_copy(
+                src_ref=wbuf.at[0, plane],
+                dst_ref=wbuf.at[0, plane],
+                send_sem=w_send.at[i],
+                recv_sem=w_recv.at[0],
+                device_id=mate,
+                device_id_type=MESH,
+            ).wait_send()
 
 
 def fused(keys, values, queries, learn_rate, w_gate, w_up, w_out):
@@ -347,11 +403,12 @@
         vmem((tokens, width), BF16),
         vmem((1, tokens), F32),
         vmem((2, db, hidden), BF16),
-        vmem((2 * hb, db), F32),
+        vmem((part_rows, db), F32),
+        vmem((part_rows, db), F32),
         vmem((2 * hb, width), F32),
         vmem((hb, width), F32),
-        vmem((planes - 1, part_rows, db), BF16),
-        vmem((planes - 1, part_rows, db), BF16),
+        vmem((3, part_rows, db), BF16),
+        vmem((4, part_rows, db), BF16),
         vmem((4, 8, db), F32),
         vmem((planes, 8, db), F32),
         vmem((2, planes, part_rows, db), BF16),
@@ -363,14 +420,14 @@
         dma((2, 3)),
         dma,
         dma,
-        dma((planes - 1,)),
-        dma((planes - 1,)),
+        dma((3,)),
+        dma((4,)),
         dma((3,)),
         dma((3,)),
         dma((planes - 1,)),
-        dma((planes - 1,)),
-        dma((planes - 1,)),
-        dma((planes - 1,)),
+        dma((planes,)),
+        dma((4,)),
+        dma((planes,)),
         dma((planes,)),
         dma((planes,)),
         dma,
@@ -442,7 +499,7 @@
     fits = (
         cores == 2
         and seq % 2 == 0
-        and planes > 1
+        and planes == 4
         and width % (128 * planes) == 0
         and hidden % (4 * 32 * planes) == 0
         and hidden // 4 == 128

time: 43 us -> 42.2 us (0.981)
  Pallas kernels: 41.3 us -> 40.5 us
    pallas_call x1, Pallas kernels: 41.3 us -> 40.5 us  [fused(): pl.pallas_call(functools.partial(kernel, planes), out_shape=jax.ShapeDtyp...]
where the time goes in v4:
time: 42.2 us; the launch traced here: 42.1 us
  Pallas kernels  40.5 us (96%)
  local copies, waits for them, and re-layouts  1.57 us (4%)
    pallas_call x1, Pallas kernels, fused(): pl.pallas_call(functools.partial(kernel, planes), out_shape=jax.ShapeDtyp...  40.5 us
    unnamed x1, local copies, waits for them, and re-layouts  1.57 us

profile of v4, /device:TPU:0, one launch (start us, length us, event | category | flops | bytes accessed | tf_op | source)
XLA Modules:
  0.0 42.1 jit_solution(1774357881079826379)
XLA Ops:
  0.0 40.5 %shard_map.73 = bf16[128,512]{1,0:T(8,128)(2,1)} custom-call(f32[1,128]{1,0:T(1,128)} %bitcast.1, bf16[128,512]{1,0:T(8,128)(2,1)} %k_ref.1, bf16[128,512]{1,0:T(8,128)(2,1)} %v_ref.1, bf16[128,512]{1,0:T(8,128)(2,1)} %q_ref.1, bf16[512,512]{1,0:T(8,128)(2,1)} %wg_ref.1, bf16[512,512]{1,0:T(8,128)(2,1)} %wu_ref.1, bf16[512,512]{1,0:T(8,128)(2,1)} %wo_ref.1), custom_call_target="tpu_custom_call" | custom-call | flops 603979776 | bytes 2097152 | tf_op jit(solution)/shard_map/pallas_call | solution.py:437
  40.5 1.6 %copy.9 = bf16[128,512]{1,0:T(8,128)(2,1)} copy(bf16[128,512]{1,0:T(8,128)(2,1)} %shard_map.73) | data formatting | bytes 262144

commit v5 on v4

--- a/solution.py
+++ b/solution.py
@@ -243,6 +243,11 @@
     gsend[0] = stacked(jnp.where(outer, far, fin)).astype(BF16)
     g_copies = [g_copy(0, jnp.where(outer, buddy, fin), jnp.where(outer, 3, 0))]
     gsend[1] = stacked(jnp.where(outer, fin, buddy)).astype(BF16)
+
+    @pl.when(outer)
+    def _():
+        g_copies[0].wait_send()
+
     g_copies.append(g_copy(1, jnp.where(outer, fin, buddy), jnp.where(outer, 1, 0)))
 
     @pl.when(outer)
@@ -368,13 +373,14 @@
     o_ref[...] = (own + precv[...].astype(F32)).astype(BF16)
 
     outgoing = [k_across, s_across, k_mate, s_mate, k_forward, s_forward, q_copy, p_copy]
-    outgoing += g_copies + w_copies + list(f_copies.values())
+    outgoing += g_copies[1:] + w_copies + list(f_copies.values())
     outgoing += st_copies + c_copies
     for copy in outgoing:
         copy.wait_send()
 
     @pl.when(inner)
     def _():
+        g_copies[0].wait_send()
         for i in (2, 3):
             pltpu.make_async_remote_copy(
                 src_ref=wbuf.at[0, plane],
@@ -441,7 +447,7 @@
         out_specs=pl.BlockSpec(memory_space=pltpu.VMEM),
         scratch_shapes=scratch,
         compiler_params=pltpu.CompilerParams(
-            collective_id=0, has_side_effects=True, vmem_limit_bytes=60 * 2**20
+            collective_id=0, has_side_effects=True, vmem_limit_bytes=215 * 2**18
         ),
         cost_estimate=pl.CostEstimate(
             flops=2 * tokens * width * hidden * 9, bytes_accessed=2 * 2**20, transcendentals=0

time: 42.2 us -> 41.7 us (0.988)
    unnamed x1 -> x3, local copies, waits for them, and re-layouts: 1.57 us -> 1.31 us
where the time goes in v5:
time: 41.7 us; the launch traced here: 41.6 us
  Pallas kernels  40.3 us (97%)
  local copies, waits for them, and re-layouts  1.31 us (3%)
    pallas_call x1, Pallas kernels, fused(): pl.pallas_call(functools.partial(kernel, planes), out_shape=jax.ShapeDtyp...  40.3 us
    unnamed x3, local copies, waits for them, and re-layouts  1.31 us

profile of v5, /device:TPU:0, one launch (start us, length us, event | category | flops | bytes accessed | tf_op | source)
XLA Modules:
  0.0 41.6 jit_solution(334393164255946625)
XLA Ops:
  0.0 0.0 copy-start
  0.0 0.7 %copy-done = f32[128]{0:T(128)S(1)} copy-done((f32[128]{0:T(128)S(1)}, f32[128]{0:T(128)}, u32[]{:S(2)}) %copy-start) | copy-done | bytes 536
  0.7 40.3 %shard_map.73 = bf16[128,512]{1,0:T(8,128)(2,1)S(1)} custom-call(f32[1,128]{1,0:T(1,128)S(1)} %bitcast.1, bf16[128,512]{1,0:T(8,128)(2,1)} %k_ref.1, bf16[128,512]{1,0:T(8,128)(2,1)} %v_ref.1, bf16[128,512]{1,0:T(8,128)(2,1)} %q_ref.1, bf16[512,512]{1,0:T(8,128)(2,1)} %wg_ref.1, bf16[512,512]{1,0:T(8,128)(2,1)} %wu_ref.1, bf16[512,512]{1,0:T(8,128)(2,1)} %wo_ref.1), custom_call_target="tpu_custom_call" | custom-call | flops 603979776 | bytes 2097152 | tf_op jit(solution)/shard_map/pallas_call | solution.py:443
  40.9 0.7 %copy.9 = bf16[128,512]{1,0:T(8,128)(2,1)} copy(bf16[128,512]{1,0:T(8,128)(2,1)S(1)} %shard_map.73) | data formatting | bytes 262144
Async XLA Ops:
  0.0 0.7 %copy-start = (f32[128]{0:T(128)S(1)}, f32[128]{0:T(128)}, u32[]{:S(2)}) copy-start(f32[128]{0:T(128)} %param.10) | copy-start | bytes 1540

commit v6 on v5

--- a/solution.py
+++ b/solution.py
@@ -160,10 +160,10 @@
             peer,
         )
 
+    k_mate = token_copy(k_ref, kbuf, 0, 1, mate)
+    s_mate = token_copy(sbuf.at[rows(0)], sbuf, 1, 1, mate)
     k_across = token_copy(k_ref, kbuf, 0, 2, across)
     s_across = token_copy(sbuf.at[rows(0)], sbuf, 1, 2, across)
-    k_mate = token_copy(k_ref, kbuf, 0, 1, mate)
-    s_mate = token_copy(sbuf.at[rows(0)], sbuf, 1, 1, mate)
     for copy in loads[2:]:
         copy.wait()
 
@@ -212,7 +212,6 @@
     last = pre(rows(3))
     s_across.wait_recv()
     s_forward = token_copy(sbuf.at[rows(2)], sbuf, 1, 3, mate)
-    q_copy = send(q_ref, qbuf.at[rows(1)], q_send, q_recv, across)
     g_in, g_out = grads(rows(2), *ready)
     acc_in[...] += g_in
     acc_out[...] += g_out
@@ -260,6 +259,7 @@
         gsend[2] = (stacked(far) + grecv[3].astype(F32)).astype(BF16)
 
     g_copies.append(g_copy(2, jnp.where(outer, buddy, far), jnp.where(outer, 2, 1)))
+    q_copy = send(q_ref, qbuf.at[rows(1)], q_send, q_recv, across)
     update[...] = old[...] + stacked(plane)
     g_arrived(0)
     update[...] += grecv[0].astype(F32)
@@ -298,12 +298,11 @@
             wbuf.at[0, p], wbuf.at[0, p], w_send.at[i], w_recv.at[p], {"seq": dst * 2 + side}
         )
 
-    w_copies = [w_copy(0, plane, jnp.where(outer, fin, buddy))]
-
     def to_mate(index, p):
         return send(wbuf.at[0, p], wbuf.at[1, p], c_send.at[index], c_recv.at[index], mate)
 
     c_copies = [to_mate(0, plane)]
+    w_copies = [w_copy(0, plane, jnp.where(outer, fin, buddy))]
 
     for copy in st_copies:
         copy.wait_recv()

time: 41.7 us -> 41.7 us (level)
  no operation moved by 1% of the time
where the time goes in v6:
time: 41.7 us; the launch traced here: 41.6 us
  Pallas kernels  40.3 us (97%)
  local copies, waits for them, and re-layouts  1.31 us (3%)
    pallas_call x1, Pallas kernels, fused(): pl.pallas_call(functools.partial(kernel, planes), out_shape=jax.ShapeDtyp...  40.3 us
    unnamed x3, local copies, waits for them, and re-layouts  1.31 us

profile of v6, /device:TPU:0, one launch (start us, length us, event | category | flops | bytes accessed | tf_op | source)
XLA Modules:
  0.0 41.6 jit_solution(7590920554092018782)
XLA Ops:
  0.0 0.0 copy-start
  0.0 0.7 %copy-done = f32[128]{0:T(128)S(1)} copy-done((f32[128]{0:T(128)S(1)}, f32[128]{0:T(128)}, u32[]{:S(2)}) %copy-start) | copy-done | bytes 536
  0.7 40.3 %shard_map.73 = bf16[128,512]{1,0:T(8,128)(2,1)S(1)} custom-call(f32[1,128]{1,0:T(1,128)S(1)} %bitcast.1, bf16[128,512]{1,0:T(8,128)(2,1)} %k_ref.1, bf16[128,512]{1,0:T(8,128)(2,1)} %v_ref.1, bf16[128,512]{1,0:T(8,128)(2,1)} %q_ref.1, bf16[512,512]{1,0:T(8,128)(2,1)} %wg_ref.1, bf16[512,512]{1,0:T(8,128)(2,1)} %wu_ref.1, bf16[512,512]{1,0:T(8,128)(2,1)} %wo_ref.1), custom_call_target="tpu_custom_call" | custom-call | flops 603979776 | bytes 2097152 | tf_op jit(solution)/shard_map/pallas_call | solution.py:442
  40.9 0.7 %copy.9 = bf16[128,512]{1,0:T(8,128)(2,1)} copy(bf16[128,512]{1,0:T(8,128)(2,1)S(1)} %shard_map.73) | data formatting | bytes 262144
Async XLA Ops:
  0.0 0.7 %copy-start = (f32[128]{0:T(128)S(1)}, f32[128]{0:T(128)}, u32[]{:S(2)}) copy-start(f32[128]{0:T(128)} %param.10) | copy-start | bytes 1540

commit v7 on v6

--- a/solution.py
+++ b/solution.py
@@ -98,6 +98,11 @@
     def same_spot(distance):
         return {"seq": plane_at(distance) * 2 + side}
 
+    barrier = pltpu.get_barrier_semaphore()
+    peers = [mate, across, diagonal] + [same_spot(d) for d in range(1, planes)]
+    for peer in peers:
+        pl.semaphore_signal(barrier, inc=1, device_id=peer, device_id_type=MESH)
+
     def rows(slot):
         return pl.ds(slot * tokens, tokens)
 
@@ -116,11 +121,6 @@
     loads = [pltpu.make_async_copy(a, b, load.at[i]) for i, (a, b) in enumerate(moves)]
     for copy in loads:
         copy.start()
-
-    barrier = pltpu.get_barrier_semaphore()
-    peers = [mate, across, diagonal] + [same_spot(d) for d in range(1, planes)]
-    for peer in peers:
-        pl.semaphore_signal(barrier, inc=1, device_id=peer, device_id_type=MESH)
 
     loads[0].wait()
     loads[1].wait()
@@ -303,15 +303,15 @@
 
     c_copies = [to_mate(0, plane)]
     w_copies = [w_copy(0, plane, jnp.where(outer, fin, buddy))]
-
-    for copy in st_copies:
-        copy.wait_recv()
     w_copies.append(w_copy(1, plane, jnp.where(outer, buddy, far)))
 
     @pl.when(inner)
     def _():
         w_copy(2, plane, fin)
 
+
+    for copy in st_copies:
+        copy.wait_recv()
     total = stat[0] + stat[1] + stat[2] + stat[3]
     olds = jnp.concatenate([jnp.broadcast_to(one, (4, db)) for one in old_sums], axis=0)
     fact[plane] = jnp.sqrt(olds / hidden + epsilon) / jnp.sqrt(total / hidden + epsilon)
@@ -340,6 +340,11 @@
         jnp.where(outer, fin, buddy),
         jnp.where(outer, far, fin),
     )
+
+    def scale_first(p):
+        arrived(fact.at[p], f_recv.at[p], mate, f_send.at[0])
+        place(0, p)
+
     for i, p in enumerate(order):
         arrived(wbuf.at[0, p], w_recv.at[p], mate, w_send.at[0])
         c_copies.append(to_mate(i + 1, p))
@@ -349,8 +354,10 @@
             def _():
                 w_copy(3, far, buddy)
 
-        arrived(fact.at[p], f_recv.at[p], mate, f_send.at[0])
-        place(0, p)
+        if i == 1:
+            scale_first(order[0])
+    scale_first(order[1])
+    scale_first(order[2])
     q_copy.wait_recv()
     for i, p in enumerate(order):
         arrived(wbuf.at[1, p], c_recv.at[i + 1], mate, c_send.at[0])
@@ -365,13 +372,21 @@
             acts.append((gate * jax.nn.sigmoid(gate) * up).astype(BF16))
         return jnp.dot(jnp.concatenate(acts, axis=1), wo[...], preferred_element_type=F32)
 
-    psend[...] = apply(slice(tokens, 2 * tokens)).astype(BF16)
-    p_copy = send(psend, precv, p_send, p_recv, across)
+    half = tokens // 2
+    p_copies = []
+    for i in range(2):
+        these = slice(i * half, (i + 1) * half)
+        psend[these, :] = apply(slice(tokens + i * half, tokens + (i + 1) * half)).astype(BF16)
+        p_copies.append(
+            send(psend.at[these], precv.at[these], p_send.at[i], p_recv.at[i], across)
+        )
     own = apply(slice(0, tokens))
-    p_copy.wait_recv()
-    o_ref[...] = (own + precv[...].astype(F32)).astype(BF16)
-
-    outgoing = [k_across, s_across, k_mate, s_mate, k_forward, s_forward, q_copy, p_copy]
+    for i in range(2):
+        these = slice(i * half, (i + 1) * half)
+        p_copies[i].wait_recv()
+        o_ref[these, :] = (own[these, :] + precv[these, :].astype(F32)).astype(BF16)
+
+    outgoing = [k_across, s_across, k_mate, s_mate, k_forward, s_forward, q_copy] + p_copies
     outgoing += g_copies[1:] + w_copies + list(f_copies.values())
     outgoing += st_copies + c_copies
     for copy in outgoing:
@@ -435,8 +450,8 @@
         dma((planes,)),
         dma((planes,)),
         dma((planes,)),
-        dma,
-        dma,
+        dma((2,)),
+        dma((2,)),
         dma((9,)),
     ]
     return pl.pallas_call(

time: 41.7 us -> 40 us (0.959)
  Pallas kernels: 40.3 us -> 38.5 us
    pallas_call x1, Pallas kernels: 40.3 us -> 38.5 us  [fused(): pl.pallas_call(functools.partial(kernel, planes), out_shape=jax.ShapeDtyp...]
where the time goes in v7:
time: 40 us; the launch traced here: 39.9 us
  Pallas kernels  38.5 us (96%)
  local copies, waits for them, and re-layouts  1.31 us (3%)
    pallas_call x1, Pallas kernels, fused(): pl.pallas_call(functools.partial(kernel, planes), out_shape=jax.ShapeDtyp...  38.5 us
    unnamed x3, local copies, waits for them, and re-layouts  1.31 us

profile of v7, /device:TPU:0, one launch (start us, length us, event | category | flops | bytes accessed | tf_op | source)
XLA Modules:
  0.0 39.9 jit_solution(720652790540995184)
XLA Ops:
  0.0 0.0 copy-start
  0.0 0.7 %copy-done = f32[128]{0:T(128)S(1)} copy-done((f32[128]{0:T(128)S(1)}, f32[128]{0:T(128)}, u32[]{:S(2)}) %copy-start) | copy-done | bytes 536
  0.7 38.5 %shard_map.73 = bf16[128,512]{1,0:T(8,128)(2,1)S(1)} custom-call(f32[1,128]{1,0:T(1,128)S(1)} %bitcast.1, bf16[128,512]{1,0:T(8,128)(2,1)} %k_ref.1, bf16[128,512]{1,0:T(8,128)(2,1)} %v_ref.1, bf16[128,512]{1,0:T(8,128)(2,1)} %q_ref.1, bf16[512,512]{1,0:T(8,128)(2,1)} %wg_ref.1, bf16[512,512]{1,0:T(8,128)(2,1)} %wu_ref.1, bf16[512,512]{1,0:T(8,128)(2,1)} %wo_ref.1), custom_call_target="tpu_custom_call" | custom-call | flops 603979776 | bytes 2097152 | tf_op jit(solution)/shard_map/pallas_call | solution.py:457
  39.2 0.7 %copy.9 = bf16[128,512]{1,0:T(8,128)(2,1)} copy(bf16[128,512]{1,0:T(8,128)(2,1)S(1)} %shard_map.73) | data formatting | bytes 262144
Async XLA Ops:
  0.0 0.7 %copy-start = (f32[128]{0:T(128)S(1)}, f32[128]{0:T(128)}, u32[]{:S(2)}) copy-start(f32[128]{0:T(128)} %param.10) | copy-start | bytes 1540

commit v8 on v7

--- a/solution.py
+++ b/solution.py
@@ -189,11 +189,14 @@
         slope = up_pre * (sigma * (1.0 + gate_pre * (1.0 - sigma)))
         return act, swish, slope
 
-    def grads(span, act, swish, slope):
+    def signals(span, swish, slope):
         back = lax.dot_general(sbuf[span, :], wback[...], NT, preferred_element_type=F32)
         d_gate = (back * slope).astype(BF16)
         d_up = (back * swish).astype(BF16)
-        both = jnp.concatenate([d_gate, d_up], axis=1)
+        return jnp.concatenate([d_gate, d_up], axis=1)
+
+    def grads(span, act, swish, slope):
+        both = signals(span, swish, slope)
         g_in = lax.dot_general(both, kbuf[span, :], TN, preferred_element_type=F32)
         g_out = lax.dot_general(act, sbuf[span, :], TN, preferred_element_type=F32)
         return g_in, g_out
@@ -216,9 +219,12 @@
     acc_in[...] += g_in
     acc_out[...] += g_out
     s_forward.wait_recv()
-    g_in, g_out = grads(rows(3), *last)
-    acc_in[...] += g_in
-    acc_out[...] += g_out
+    act, swish, slope = last
+    both = signals(rows(3), swish, slope)
+    acc_out[...] += lax.dot_general(act, sbuf[rows(3), :], TN, preferred_element_type=F32)
+    lead = jnp.where(outer, far, fin)
+    lead_cols = pl.ds(pl.multiple_of(lead * db, db), db)
+    lead_in = lax.dot_general(both, kbuf[rows(3), lead_cols], TN, preferred_element_type=F32)
 
     def part(p):
         return acc_in[:, pl.ds(pl.multiple_of(p * db, db), db)], acc_out[
@@ -239,14 +245,13 @@
     def g_arrived(slot):
         arrived(grecv.at[slot], g_recv.at[slot], mate, g_send.at[0])
 
-    gsend[0] = stacked(jnp.where(outer, far, fin)).astype(BF16)
+    lead_top, lead_low = part(lead)
+    gsend[0] = jnp.concatenate(
+        [lead_top + lead_in] + [lead_low[:, j * db : (j + 1) * db] for j in range(spread)], axis=0
+    ).astype(BF16)
     g_copies = [g_copy(0, jnp.where(outer, buddy, fin), jnp.where(outer, 3, 0))]
+    acc_in[...] += lax.dot_general(both, kbuf[rows(3), :], TN, preferred_element_type=F32)
     gsend[1] = stacked(jnp.where(outer, fin, buddy)).astype(BF16)
-
-    @pl.when(outer)
-    def _():
-        g_copies[0].wait_send()
-
     g_copies.append(g_copy(1, jnp.where(outer, fin, buddy), jnp.where(outer, 1, 0)))
 
     @pl.when(outer)
@@ -387,14 +392,13 @@
         o_ref[these, :] = (own[these, :] + precv[these, :].astype(F32)).astype(BF16)
 
     outgoing = [k_across, s_across, k_mate, s_mate, k_forward, s_forward, q_copy] + p_copies
-    outgoing += g_copies[1:] + w_copies + list(f_copies.values())
+    outgoing += g_copies + w_copies + list(f_copies.values())
     outgoing += st_copies + c_copies
     for copy in outgoing:
         copy.wait_send()
 
     @pl.when(inner)
     def _():
-        g_copies[0].wait_send()
         for i in (2, 3):
             pltpu.make_async_remote_copy(
                 src_ref=wbuf.at[0, plane],

time: 40 us -> 39.5 us (0.988)
    pallas_call x1, Pallas kernels: 38.5 us -> 38.1 us  [fused(): pl.pallas_call(functools.partial(kernel, planes), out_shape=jax.ShapeDtyp...]
where the time goes in v8:
time: 39.5 us; the launch traced here: 39.4 us
  Pallas kernels  38.1 us (96%)
  local copies, waits for them, and re-layouts  1.31 us (3%)
    pallas_call x1, Pallas kernels, fused(): pl.pallas_call(functools.partial(kernel, planes), out_shape=jax.ShapeDtyp...  38.1 us
    unnamed x3, local copies, waits for them, and re-layouts  1.31 us

profile of v8, /device:TPU:0, one launch (start us, length us, event | category | flops | bytes accessed | tf_op | source)
XLA Modules:
  0.0 39.4 jit_solution(8585402100930353936)
XLA Ops:
  0.0 0.0 copy-start
  0.0 0.7 %copy-done = f32[128]{0:T(128)S(1)} copy-done((f32[128]{0:T(128)S(1)}, f32[128]{0:T(128)}, u32[]{:S(2)}) %copy-start) | copy-done | bytes 536
  0.7 38.1 %shard_map.73 = bf16[128,512]{1,0:T(8,128)(2,1)S(1)} custom-call(f32[1,128]{1,0:T(1,128)S(1)} %bitcast.1, bf16[128,512]{1,0:T(8,128)(2,1)} %k_ref.1, bf16[128,512]{1,0:T(8,128)(2,1)} %v_ref.1, bf16[128,512]{1,0:T(8,128)(2,1)} %q_ref.1, bf16[512,512]{1,0:T(8,128)(2,1)} %wg_ref.1, bf16[512,512]{1,0:T(8,128)(2,1)} %wu_ref.1, bf16[512,512]{1,0:T(8,128)(2,1)} %wo_ref.1), custom_call_target="tpu_custom_call" | custom-call | flops 603979776 | bytes 2097152 | tf_op jit(solution)/shard_map/pallas_call | solution.py:461
  38.7 0.7 %copy.9 = bf16[128,512]{1,0:T(8,128)(2,1)} copy(bf16[128,512]{1,0:T(8,128)(2,1)S(1)} %shard_map.73) | data formatting | bytes 262144
Async XLA Ops:
  0.0 0.7 %copy-start = (f32[128]{0:T(128)S(1)}, f32[128]{0:T(128)}, u32[]{:S(2)}) copy-start(f32[128]{0:T(128)} %param.10) | copy-start | bytes 1540
